TPU v7x, 256 devices: a whole 4x4x8 slice. The times are simulated.
256 devices in a mesh: ctx: 16 (over x_lo, y, core), head: 16 (over z, x_hi).
Axes of the slice: x: 4 (x_hi: 2, x_lo: 2; x = x_hi * 2 + x_lo), y: 4, z: 8, core: 2. Of those that a mesh axis runs over, the one named last changes fastest.
Arguments:
- tokens: bfloat16 [16384, 5376], P('ctx', 'head'), may hold values from -48 to 48
- w_qkv: bfloat16 [5376, 8192], P('ctx', 'head')
Outputs:
- attended: bfloat16 [16384, 4096], P('ctx', 'head')
All inputs are finite; a program needn't handle non-finite values.
Results may differ from a plain program's by a relative error of at most 0.011.
Values may be sent and summed in bfloat16 or wider, within the bound.
No kernel may reach another device: no remote copies, remote signals or barrier semaphores. Data moves between devices by JAX's collectives and lax.ppermute only.
A program may use at most 128 MiB of HBM per device.

v0:
```python
import jax
import jax.numpy as jnp
from jax import lax
from jax.sharding import PartitionSpec as P

HEAD_DIM = 128
Q_PER_KV = 2
WINDOW = 1024
rope_base = 10000.0
query_scale = 168.0 ** (-0.5)
masked_score = -1e30


def passed_along(block, axis, distance):
    devices = range(lax.axis_size(axis))
    route = [(i - distance, i) for i in devices if i - distance in devices]
    return lax.ppermute(block, axis, route)


def rotate(projected, positions):
    head_width = projected.shape[-1]
    half_width = head_width // 2
    inverse = jnp.power(rope_base, -2.0 * jnp.arange(half_width, dtype=jnp.float32) / head_width)
    angles = positions.astype(jnp.float32)[:, None] * inverse[None, :]
    target_shape = (projected.shape[0],) + (1,) * (projected.ndim - 2) + (half_width,)
    cosine = jnp.cos(angles).reshape(target_shape)
    sine_part = jnp.sin(angles).reshape(target_shape)
    leading = projected[..., :half_width]
    second = projected[..., half_width:]
    return jnp.concatenate(
        [leading * cosine - second * sine_part, second * cosine + leading * sine_part], axis=-1
    )


def add_rows(left_rows, shard_rows):
    return jnp.dot(left_rows, shard_rows, preferred_element_type=jnp.float32)


def extend(key_rows, value_rows):
    stacked = jnp.stack([key_rows, value_rows], axis=0)
    border = passed_along(stacked, "ctx", 1)
    return (
        jnp.concatenate([border[0], key_rows], axis=0),
        jnp.concatenate([border[1], value_rows], axis=0),
    )


def attend(queries, key_rows, value_rows, key_anchor):
    row_count = queries.shape[0]
    block_rows = min(512, row_count)
    span = key_rows.shape[0] - row_count
    query_pos = jnp.arange(block_rows, dtype=jnp.int32)[:, None]
    key_pos = jnp.arange(block_rows + span, dtype=jnp.int32)[None, :]

    def one_block(block_index):
        first_row = block_index * block_rows
        query_block = lax.dynamic_slice_in_dim(queries, first_row, block_rows, 0)
        key_block = lax.dynamic_slice_in_dim(key_rows, first_row, block_rows + span, 0)
        value_block = lax.dynamic_slice_in_dim(value_rows, first_row, block_rows + span, 0)
        scores = (
            jnp.einsum("qkgd,ckd->kgqc", query_block, key_block, preferred_element_type=jnp.float32)
            * query_scale
        )
        allowed = (
            (key_pos > query_pos)
            & (key_pos <= query_pos + span)
            & (key_anchor + first_row + key_pos >= 0)
        )
        scores = jnp.where(allowed[None, None], scores, masked_score)
        highest = jnp.max(scores, axis=-1, keepdims=True)
        expanded = jnp.exp(scores - highest)
        probabilities = (expanded / jnp.sum(expanded, axis=-1, keepdims=True)).astype(jnp.bfloat16)
        summed = jnp.einsum(
            "kgqc,ckd->qkgd", probabilities, value_block, preferred_element_type=jnp.float32
        )
        return summed.astype(jnp.bfloat16)

    attended = lax.map(one_block, jnp.arange(row_count // block_rows, dtype=jnp.int32))
    return attended.reshape(row_count, -1)


def on_device(tokens, w_qkv):
    row_count = tokens.shape[0]
    groups = w_qkv.shape[1] // ((Q_PER_KV + 2) * HEAD_DIM)
    device_index = lax.axis_index("ctx")
    positions = device_index * row_count + jnp.arange(row_count, dtype=jnp.int32)
    key_anchor = device_index * row_count - WINDOW
    gathered = lax.all_gather(tokens, "head", axis=1, tiled=True)
    projected = add_rows(gathered, lax.all_gather(w_qkv, "ctx", axis=0, tiled=True))
    projected = projected.reshape(row_count, groups, Q_PER_KV + 2, HEAD_DIM)
    queries = rotate(projected[:, :, :Q_PER_KV], positions).astype(jnp.bfloat16)
    key_rows = rotate(projected[:, :, Q_PER_KV], positions).astype(jnp.bfloat16)
    value_rows = projected[:, :, Q_PER_KV + 1].astype(jnp.bfloat16)
    key_rows, value_rows = extend(key_rows, value_rows)
    return attend(queries, key_rows, value_rows, key_anchor)


def solution(mesh):
    placed = (P("ctx", "head"), P("ctx", "head"))
    return jax.shard_map(
        on_device, mesh=mesh, in_specs=placed, out_specs=P("ctx", "head"), check_vma=False
    )
```

profile of v0, /device:TPU:2, one launch (start us, length us, event | category | flops | bytes accessed | tf_op | source)
XLA Modules:
  0.0 274.9 jit_solution(17137558417569004634)
XLA Ops:
  6.5 0.7 all-gather.5.cloned.1.call-update
  7.3 0.7 all-gather.3.cloned.1.call-update
  8.1 3.1 %multiply_cosine_fusion = (f32[1024,64]{1,0:T(8,128)}, f32[1024,64]{1,0:T(8,128)}) fusion(f32[64]{0:T(128)S(1)} %multiply_power_fusion, f32[1024]{0:T(1024)S(1)} %add_convert_fusion.1), kind=kLoop, calls=%fused_computation.33 | loop fusion | flops 65536 | bytes 528640 | tf_op jit(solution)/shard_map/cos | solution.py:26
  11.1 43.1 %all-gather.5.cloned.1.call-done = bf16[5376,512]{1,0:T(8,128)(2,1)} async-done(((bf16[336,512]{1,0:T(8,128)(2,1)}), bf16[5376,512]{1,0:T(8,128)(2,1)}) %all-gather.5.cloned.1.call-update) | async-done | bytes 5505040 | tf_op jit(solution)/shard_map/all_gather | solution.py:89
  54.3 164.7 %all-gather.3.cloned.1.call-done = bf16[1024,5376]{0,1:T(8,128)(2,1)} async-done(((bf16[1024,336]{0,1:T(8,128)(2,1)}), bf16[1024,5376]{0,1:T(8,128)(2,1)}) %all-gather.3.cloned.1.call-update) | async-done | bytes 11010064 | tf_op jit(solution)/shard_map/all_gather | solution.py:88
  219.0 10.3 %fusion.37 = f32[1024,512]{0,1:T(8,128)S(1)} fusion(bf16[1024,5376]{0,1:T(8,128)(2,1)} %all-gather.3.cloned.1.call-done, bf16[5376,512]{1,0:T(8,128)(2,1)} %all-gather.5.cloned.1.call-done), kind=kOutput, calls=%fused_computation.56 | convolution fusion | flops 5637144576 | bytes 18612224 | tf_op jit(solution)/shard_map/dot_general | solution.py:36
  229.4 1.3 copy-done
  230.9 2.4 fusion.33
  233.5 1.0 pad_maximum_fusion
  234.4 2.1 collective-permute-start
  236.5 1.3 fusion.36
  237.8 0.3 copy.23
  238.1 0.3 copy.24
  238.5 1.5 subtract_convert_fusion
  240.0 0.3 pad_maximum_fusion.2
  240.3 7.1 %collective-permute-done = bf16[2,1024,1,128]{3,1,2,0:T(8,128)(2,1)} collective-permute-done((bf16[2,1024,1,128]{3,1,2,0:T(8,128)(2,1)}, bf16[2,1024,1,128]{3,1,2,0:T(8,128)(2,1)}, u32[]{:S(2)}, u32[]{:S(2)}) %collective-permute-start) | collective-permute-done | bytes 524320 | tf_op jit(solution)/shard_map/ppermute | solution.py:17
  247.3 1.1 slice_bitcast_fusion
  248.6 17.6 %while.12 = (s32[]{:T(128)}, bf16[2,512,1,2,128]{4,3,1,0,2:T(2,128)(2,1)}, s32[2]{0:T(128)S(1)}, bf16[2048,1,128]{2,0,1:T(8,128)(2,1)S(1)}, s32[]{:T(128)}, /*in...) while((s32[]{:T(128)}, ...), condition=%wide.region_3.4_spmd.clone.clone, body=%wide.region_0.3_spmd.clone.clone.sunk | while | flops 827459072 | bytes 28601632 | solution.py:78
  248.6 0.6 dynamic_slice.44
  249.9 1.3 fusion.50
  251.1 1.4 fusion.51
  252.5 1.4 fusion.52
  254.0 2.2 fusion.53
  256.6 0.8 copy-done.2
  257.4 0.6 dynamic_slice.44
  258.6 1.3 fusion.50
  259.9 1.4 fusion.51
  261.3 1.4 fusion.52
  262.8 2.2 fusion.53
  265.1 0.2 constant_dynamic-update-slice_fusion.2
  265.4 0.8 copy-done.2
  266.1 1.9 copy.27
  (25 shorter events, 1.2 us)
Async XLA Ops:
  6.5 47.7 %all-gather.5.cloned.1.call-start = ((), (), s32[]{:S(2)}) async-start(), calls=%async_computation.1 | async-start | bytes 5849088 | tf_op jit(solution)/shard_map/all_gather | solution.py:89
  7.3 211.7 %all-gather.3.cloned.1.call-start = ((), (), s32[]{:S(2)}) async-start(), calls=%async_computation | async-start | bytes 11698176 | tf_op jit(solution)/shard_map/all_gather | solution.py:88
  229.3 1.3 copy-start
  234.4 12.9 %collective-permute-start = (bf16[2,1024,1,128]{3,1,2,0:T(8,128)(2,1)}, bf16[2,1024,1,128]{3,1,2,0:T(8,128)(2,1)}, u32[]{:S(2)}, u32[]{:S(2)}) collective-permute-start(bf16[2,1024,1,128]{3,1,2,0:T(8,128)(2,1)} %pad_maximum_fusion), channel_id=1, source_target_pairs={{0,16},{16,32},{32,48},{48,64},{64,80},{80,96},{96,112},{112,128},... | collective-permute-start | bytes 1572872 | tf_op jit(solution)/shard_map/ppermute | solution.py:17
  254.0 2.4 copy-start.1
  256.6 0.8 copy-start.2
  262.7 2.4 copy-start.1
  265.3 0.8 copy-start.2
Sparse Core Ops, SparseCore 0:
  9.2 45.0 all-gather.4
  56.9 162.0 all-gather.2
where the time goes:
time: 275 us
  waiting for transfers between devices  216 us (79%)
  matrix products  17.5 us (6%)
  other arithmetic  13.8 us (5%)
  between operations  13.5 us (5%)
  local copies, waits for them, and re-layouts  10.1 us (4%)
    all_gather x1, waiting for transfers between devices, on_device(): gathered = lax.all_gather(tokens, 'head', axis=1, tiled=True)  165 us
    all_gather x1, waiting for transfers between devices, on_device(): lax.all_gather(w_qkv, 'ctx', axis=0, tiled=True)  43.1 us
    dot_general x1, matrix products, add_rows(): return jnp.dot(left_rows, shard_rows, preferred_element_type=jnp.float32)  10.3 us
    ppermute x1, waiting for transfers between devices, passed_along(): return lax.ppermute(block, axis, route)  7.08 us
  transfers between devices with their start and end apart: 3, of which 3 were waited for; matrix products, arithmetic and copies ran while one was open for 2% of the time, Pallas kernels for 0%

commit v1 on v0

--- a/solution.py
+++ b/solution.py
@@ -86,7 +86,16 @@
     positions = device_index * row_count + jnp.arange(row_count, dtype=jnp.int32)
     key_anchor = device_index * row_count - WINDOW
     gathered = lax.all_gather(tokens, "head", axis=1, tiled=True)
-    projected = add_rows(gathered, lax.all_gather(w_qkv, "ctx", axis=0, tiled=True))
+    carry_circles = lambda message: jnp.concatenate(
+        lax.all_to_all(
+            jnp.stack([message] * lax.axis_size("ctx")),
+            axis_name="ctx",
+            split_axis=0,
+            concat_axis=0,
+        ),
+        axis=0,
+    )
+    projected = add_rows(gathered, carry_circles(w_qkv))
     projected = projected.reshape(row_count, groups, Q_PER_KV + 2, HEAD_DIM)
     queries = rotate(projected[:, :, :Q_PER_KV], positions).astype(jnp.bfloat16)
     key_rows = rotate(projected[:, :, Q_PER_KV], positions).astype(jnp.bfloat16)

time: 275 us -> 248 us (0.902)
  waiting for transfers between devices: 216 us -> 181 us
  starting transfers between devices: 2.13 us -> 8.6 us
  other arithmetic: 13.8 us -> 7.92 us
  local copies, waits for them, and re-layouts: 10.1 us -> 15 us
    all_to_all x0 -> x1, waiting for transfers between devices: none -> 87 us  [on_device(): lax.all_to_all(jnp.stack([message] * lax.axis_size('ctx')), axis_name='ct...]
    all_gather x1, waiting for transfers between devices: 165 us -> 84 us  [on_device(): gathered = lax.all_gather(tokens, 'head', axis=1, tiled=True)]
    all_gather x1 -> x0, waiting for transfers between devices: 43.1 us -> none  [on_device(): lax.all_gather(w_qkv, 'ctx', axis=0, tiled=True)]
    dot_general x0 -> x1, local copies, waits for them, and re-layouts: none -> 8.02 us  [add_rows(): return jnp.dot(left_rows, shard_rows, preferred_element_type=jnp.float32)]
    all_to_all x0 -> x1, starting transfers between devices: none -> 6.68 us  [on_device(): lax.all_to_all(jnp.stack([message] * lax.axis_size('ctx')), axis_name='ct...]
    another operation x0 -> x1, local copies, waits for them, and re-layouts: none -> 3.89 us  [on_device(): jnp.stack([message] * lax.axis_size('ctx'))]
    unnamed x7 -> x1, local copies, waits for them, and re-layouts: 4.22 us -> 0.88 us
  transfers between devices with their start and end apart: 3 -> 3, of which waited for: 3 -> 3; matrix products, arithmetic and copies ran while one was open for 2% -> 5% of each run, Pallas kernels for 0% -> 0%
where the time goes in v1:
time: 248 us; the launch traced here: 245 us
  waiting for transfers between devices  181 us (73%)
  matrix products  17.6 us (7%)
  local copies, waits for them, and re-layouts  15 us (6%)
  between operations  13.5 us (5%)
  starting transfers between devices  8.6 us (3%)
  other arithmetic  7.92 us (3%)
    all_to_all x1, waiting for transfers between devices, on_device(): lax.all_to_all(jnp.stack([message] * lax.axis_size('ctx')), axis_name='ct...  87 us
    all_gather x1, waiting for transfers between devices, on_device(): gathered = lax.all_gather(tokens, 'head', axis=1, tiled=True)  84 us
    dot_general x1, matrix products, add_rows(): return jnp.dot(left_rows, shard_rows, preferred_element_type=jnp.float32)  10.3 us
    ppermute x1, waiting for transfers between devices, passed_along(): return lax.ppermute(block, axis, route)  9.46 us
    dot_general x1, local copies, waits for them, and re-layouts, add_rows(): return jnp.dot(left_rows, shard_rows, preferred_element_type=jnp.float32)  8.02 us
    all_to_all x1, starting transfers between devices, on_device(): lax.all_to_all(jnp.stack([message] * lax.axis_size('ctx')), axis_name='ct...  6.68 us
  transfers between devices with their start and end apart: 3, of which 3 were waited for; matrix products, arithmetic and copies ran while one was open for 5% of the time, Pallas kernels for 0%

profile of v1, /device:TPU:2, one launch (start us, length us, event | category | flops | bytes accessed | tf_op | source)
XLA Modules:
  0.0 245.3 jit_solution(4412483296459010649)
XLA Ops:
  6.5 0.0 all-gather.2.cloned.1.call-start
  6.5 0.7 all-gather.2.cloned.1.call-update
  7.3 3.9 %stack.4 = bf16[16,336,512]{2,1,0:T(8,128)(2,1)} broadcast(bf16[336,512]{1,0:T(8,128)(2,1)} %param.5), dimensions={1,2} | broadcast | bytes 5849088 | tf_op jit(solution)/shard_map/stack | solution.py:91
  11.1 6.7 %all-to-all-start = ((bf16[16,336,512]{2,1,0:T(8,128)(2,1)}), bf16[16,336,512]{2,1,0:T(8,128)(2,1)}, u32[]{:S(2)}, u32[]{:S(2)}) async-start(bf16[16,336,512]{2,1,0:T(8,128)(2,1)} %stack.4), calls=%async_computation | async-start | bytes 11010048 | tf_op jit(solution)/shard_map/all_to_all | solution.py:90
  17.9 87.0 %all-to-all-done = bf16[16,336,512]{2,1,0:T(8,128)(2,1)} async-done(((bf16[16,336,512]{2,1,0:T(8,128)(2,1)}), bf16[16,336,512]{2,1,0:T(8,128)(2,1)}, u32[]{:S(2)}, u32[]{:S(2)}) %all-to-all-start) | async-done | bytes 5505056 | tf_op jit(solution)/shard_map/all_to_all | solution.py:90
  104.9 8.0 %copy.9 = bf16[512,5376]{1,0:T(8,128)(2,1)} copy(bf16[512,5376]{0,1:T(8,128)(2,1)} %bitcast.2) | data formatting | bytes 11010048 | tf_op jit(solution)/shard_map/dot_general | solution.py:36
  112.9 84.0 %all-gather.2.cloned.1.call-done = bf16[1024,5376]{0,1:T(8,128)(2,1)} async-done(((bf16[1024,336]{0,1:T(8,128)(2,1)}), bf16[1024,5376]{0,1:T(8,128)(2,1)}) %all-gather.2.cloned.1.call-update) | async-done | bytes 11010064 | tf_op jit(solution)/shard_map/all_gather | solution.py:88
  196.9 10.3 %fusion.30 = f32[1024,1,4,128]{0,3,2,1:T(8,128)S(1)} fusion(bf16[4,128,5376]{2,1,0:T(8,128)(2,1)} %bitcast.96, bf16[1024,5376]{0,1:T(8,128)(2,1)} %all-gather.2.cloned.1.call-done), kind=kOutput, calls=%fused_computation.32 | convolution fusion | flops 5637144576 | bytes 18612224 | tf_op jit(solution)/shard_map/dot_general | solution.py:36
  207.3 1.2 fusion.38
  208.5 1.9 collective-permute-start
  210.4 1.0 multiply_cosine_fusion
  211.4 0.2 subtract_convert_fusion
  211.6 9.5 %collective-permute-done = bf16[2,1024,1,128]{1,3,2,0:T(8,128)(2,1)S(1)} collective-permute-done((bf16[2,1024,1,128]{1,3,2,0:T(8,128)(2,1)S(1)}, bf16[2,1024,1,128]{1,3,2,0:T(8,128)(2,1)S(1)}, u32[]{:S(2)}, u32[]{:S(2)}) %collective-permute-start) | collective-permute-done | bytes 524320 | tf_op jit(solution)/shard_map/ppermute | solution.py:17
  221.1 0.1 pad_maximum_fusion.1
  221.2 16.3 %while.12 = (s32[]{:T(128)}, bf16[2,512,1,2,128]{4,3,1,0,2:T(2,128)(2,1)S(1)}, s32[2]{0:T(128)S(1)}, bf16[2048,1,128]{0,2,1:T(8,128)(2,1)S(1)}, s32[]{:T(128)}, ...) while((s32[]{:T(128)}, ...), condition=%wide.region_3.4_spmd.clone.clone, body=%wide.region_0.3_spmd.clone.clone.sunk | while | flops 827459072 | bytes 24407272 | solution.py:78
  221.3 0.7 dynamic_slice.44
  222.6 1.3 fusion.54
  223.9 1.5 fusion.55
  225.4 1.4 fusion.56
  226.8 2.2 fusion.57
  229.0 0.2 copy.22
  229.2 0.2 constant_dynamic-update-slice_fusion.2
  229.4 0.7 dynamic_slice.44
  230.8 1.3 fusion.54
  232.0 1.5 fusion.55
  233.5 1.4 fusion.56
  235.0 2.2 fusion.57
  237.1 0.2 copy.22
  237.3 0.2 constant_dynamic-update-slice_fusion.2
  237.5 0.9 copy.20
  (13 shorter events, 0.2 us)
Async XLA Ops:
  6.5 190.3 %all-gather.2.cloned.1.call-start = ((), (), s32[]{:S(2)}) async-start(), calls=%async_computation.1 | async-start | bytes 11698176 | tf_op jit(solution)/shard_map/all_gather | solution.py:88
  11.1 93.7 %all-to-all-start = ((bf16[16,336,512]{2,1,0:T(8,128)(2,1)}), bf16[16,336,512]{2,1,0:T(8,128)(2,1)}, u32[]{:S(2)}, u32[]{:S(2)}) async-start(bf16[16,336,512]{2,1,0:T(8,128)(2,1)} %stack.4), calls=%async_computation | async-start | bytes 11010048 | tf_op jit(solution)/shard_map/all_to_all | solution.py:90
  208.5 12.6 %collective-permute-start = (bf16[2,1024,1,128]{1,3,2,0:T(8,128)(2,1)S(1)}, bf16[2,1024,1,128]{1,3,2,0:T(8,128)(2,1)S(1)}, u32[]{:S(2)}, u32[]{:S(2)}) collective-permute-start(bf16[2,1024,1,128]{1,3,2,0:T(8,128)(2,1)S(1)} %pad_maximum_fusion), channel_id=1, source_target_pairs={{0,16},{16,32},{32,48},{48,64},{64,80},{80,96},{96,112},{112,128},... | collective-permute-start | bytes 1572872 | tf_op jit(solution)/shard_map/ppermute | solution.py:17
Sparse Core Ops, SparseCore 0:
  9.9 186.8 all-gather.1
